TPU v7x, 32 devices: a whole 2x2x4 slice. The times are simulated.
32 devices in a mesh: row: 4 (over x, core), col: 8 (over z, y).
Axes of the slice: x: 2, y: 2, z: 4, core: 2. Of those that a mesh axis runs over, the one named last changes fastest.
Arguments:
- object_tiles: float32 [2, 2, 512, 1024], P(None, None, 'row', 'col'), may hold values from -3 to 3
- positions: int32 [4, 8, 6, 2], P('row', 'col'), may hold values from 0 to 128, as said below
- probe: float32 [2, 128, 128], replicated, may hold values from -4.2 to 4.2
- phase: float32 [128, 128], replicated, may hold values from -3.140625 to 3.140625
- intensity: float32 [4, 8, 6, 128, 128], P('row', 'col'), may hold values from 0.05 to 1
Outputs:
- updated_tiles: float32 [2, 2, 1024, 2048], P(None, None, 'row', 'col')
Inputs may be any that keep to these rules, and one draw needn't show every extreme that they name: `positions`: every window of 128 x 128 pixels lies inside the object. In every tile probe 0 takes the least and probe 1 the greatest row offset that this allows, probe 2 the least and probe 3 the greatest column offset.
All inputs are finite; a program needn't handle non-finite values.
Results may differ from a plain program's by a relative error of at most 0.0003.
Values sent between devices are 32-bit elements; how exact they have to be, the bound alone decides.
A program may use at most 64 MiB of HBM per device.

v0:
```python
import functools
import math

import jax
import jax.numpy as jnp
import ml_dtypes
import numpy as np
from jax import lax
from jax.experimental import pallas as pl
from jax.experimental.pallas import tpu as pltpu
from jax.sharding import PartitionSpec as P

step_size = 2.0
MESH = pl.DeviceIdType.MESH
IN_H, IN_VC, IN_VH, G_V, G_H, U_H, U_V = range(7)
LOW, HIGH = 0, 1


def dft_tables(length):
    counter = np.arange(length)
    angles = 2.0 * math.pi / length * (counter[:, None] * counter[None, :] % length)
    cos_part = np.cos(angles) / math.sqrt(length)
    sin_part = -np.sin(angles) / math.sqrt(length)
    right = np.block([[cos_part, sin_part], [-sin_part, cos_part]])
    both = np.stack([right, right.T]).astype(np.float32)
    high = both.astype(ml_dtypes.bfloat16)
    low = (both - high.astype(np.float32)).astype(ml_dtypes.bfloat16)
    return np.stack([high, low], 1)


def split(value):
    high = value.astype(jnp.bfloat16)
    low = (value - high.astype(jnp.float32)).astype(jnp.bfloat16)
    return high, low


def dot(a, b):
    return jnp.dot(a, b, preferred_element_type=jnp.float32)


def times(a, b):
    return (a[0] * b[0] - a[1] * b[1], a[0] * b[1] + a[1] * b[0])


def conj_times(a, b):
    return (a[0] * b[0] + a[1] * b[1], a[0] * b[1] - a[1] * b[0])


def kernel(
    rows, cols, pos_ref, obj_ref, probe_ref, phase_ref, meas_ref, table_ref, out_ref,
    send_h, recv_h, side, vert_c, vert_h, shifted, prop, inner, wave,
    grad, recv_gv, send_gh, recv_gh, send_uh, recv_uh, ready, zero,
    send_sem, recv_sem, local_sem, edge_sem,
):
    length = probe_ref.shape[1]
    half = length // 2
    count = pos_ref.shape[0]
    row, col = lax.axis_index("row"), lax.axis_index("col")
    lane = lax.broadcasted_iota(jnp.int32, (length, length), 1)
    line = lax.broadcasted_iota(jnp.int32, (length, length), 0)
    low_lanes = lane < half

    above, below = (row - 1, col), (row + 1, col)
    left, right = (row, col - 1), (row, col + 1)
    exists = ((row > 0, row < rows - 1), (col > 0, col < cols - 1))
    places = ((above, below), (left, right))

    def swap(value):
        return pltpu.roll(value, half, 1)

    def pack(re, im):
        return jnp.where(low_lanes, re, swap(im)), jnp.where(low_lanes, swap(re), im)

    def joined(low_pack, high_pack):
        return (
            jnp.where(low_lanes, low_pack, swap(high_pack)),
            jnp.where(low_lanes, swap(low_pack), high_pack),
        )

    def remote(kind, s, way, source, target):
        axis = 1 if kind in (IN_H, G_H, U_H) else 0
        return pltpu.make_async_remote_copy(
            src_ref=source, dst_ref=target,
            send_sem=send_sem.at[kind, s, way], recv_sem=recv_sem.at[kind, s, way],
            device_id=places[axis][way], device_id_type=MESH,
        )

    def copies(kind, s, way):
        top, bottom = pl.ds(0, half), pl.ds(half, half)
        part = top if way == LOW else bottom
        other = bottom if way == LOW else top
        if kind == IN_H:
            pair = send_h.at[s, way], recv_h.at[s, way]
        elif kind == IN_VC:
            pair = obj_ref.at[s, :, part], vert_c.at[s, :, part]
        elif kind == IN_VH:
            pair = side.at[s, :, part], vert_h.at[s, :, part]
        elif kind == G_V:
            pair = grad.at[s, 1, :, :, other], recv_gv.at[s, :, :, other]
        elif kind == G_H:
            pair = send_gh.at[s, way], recv_gh.at[s, way]
        elif kind == U_H:
            pair = send_uh.at[s, way], recv_uh.at[s, way]
        else:
            place = pl.ds(half + length, half) if way == LOW else pl.ds(0, half)
            pair = ready.at[s, :, part], out_ref.at[s, :, place]
        return remote(kind, s, way, *pair)

    def axis_of(kind):
        return 1 if kind in (IN_H, G_H, U_H) else 0

    def start(kind, s):
        for way in (LOW, HIGH):
            @pl.when(exists[axis_of(kind)][way])
            def _():
                copies(kind, s, way).start()

    def arrive(kind, s):
        for way in (LOW, HIGH):
            @pl.when(exists[axis_of(kind)][1 - way])
            def _():
                copies(kind, s, way).wait_recv()

    def leave(kind, s):
        for way in (LOW, HIGH):
            @pl.when(exists[axis_of(kind)][way])
            def _():
                copies(kind, s, way).wait_send()

    recv_gv[...] = jnp.zeros_like(recv_gv)
    recv_gh[...] = jnp.zeros_like(recv_gh)
    recv_uh[...] = jnp.zeros_like(recv_uh)
    zero[...] = jnp.zeros_like(zero)

    barrier = pltpu.get_barrier_semaphore()
    for axis in (0, 1):
        for way in (LOW, HIGH):
            @pl.when(exists[axis][way])
            def _():
                pl.semaphore_signal(barrier, inc=1, device_id=places[axis][way], device_id_type=MESH)
    for s in (0, 1):
        send_h[s, LOW], send_h[s, HIGH] = pack(obj_ref[s, 0], obj_ref[s, 1])
    peers = sum(there.astype(jnp.int32) for pair in exists for there in pair)
    pl.semaphore_wait(barrier, peers)

    start(IN_H, 0)
    start(IN_VC, 0)
    start(IN_H, 1)
    start(IN_VC, 1)

    for way in (LOW, HIGH):
        @pl.when(jnp.logical_not(exists[0][way]))
        def _():
            place = pl.ds(0, half) if way == LOW else pl.ds(half + length, half)
            pltpu.make_async_copy(zero, out_ref.at[:, :, place], edge_sem.at[way]).start()

    for number in range(count):
        down = (pos_ref[number, 0] + half) % length
        across = (pos_ref[number, 1] + half) % length
        for part in (0, 1):
            moved = pltpu.roll(probe_ref[part], down, 0)
            shifted[number, part] = pltpu.roll(moved, across, 1)
    prop[0] = jnp.cos(phase_ref[...])
    prop[1] = jnp.sin(phase_ref[...])

    for s in (0, 1):
        arrive(IN_H, s)
        side[s, 0], side[s, 1] = joined(recv_h[s, LOW], recv_h[s, HIGH])
        start(IN_VH, s)

    def masks(number):
        down, across = pos_ref[number, 0] - half, pos_ref[number, 1] - half
        in_rows = (line >= down) & (line < down + length)
        in_cols = (lane >= across) & (lane < across + length)
        return in_rows, in_cols

    def window(s, number):
        in_rows, in_cols = masks(number)
        return tuple(
            jnp.where(
                in_rows,
                jnp.where(in_cols, obj_ref[s, part], side[s, part]),
                jnp.where(in_cols, vert_c[s, part], vert_h[s, part]),
            )
            for part in (0, 1)
        )

    def from_right(pair, way):
        (a_re, a_im), (b_re, b_im) = pair
        high, low = split(
            jnp.concatenate(
                [jnp.concatenate([a_re, a_im], 1), jnp.concatenate([b_re, b_im], 1)], 0
            )
        )
        th, tl = table_ref[way, 0], table_ref[way, 1]
        y = dot(high, th) + dot(low, th) + dot(high, tl)
        return (
            (y[:length, :length], y[:length, length:]),
            (y[length:, :length], y[length:, length:]),
        )

    def from_left(pair, way):
        (a_re, a_im), (b_re, b_im) = pair
        high, low = split(
            jnp.concatenate(
                [jnp.concatenate([a_re, b_re], 1), jnp.concatenate([a_im, b_im], 1)], 0
            )
        )
        th, tl = table_ref[1 - way, 0], table_ref[1 - way, 1]
        y = dot(th, high) + dot(th, low) + dot(tl, high)
        return (
            (y[:length, :length], y[length:, :length]),
            (y[:length, length:], y[length:, length:]),
        )

    def forward(pair):
        return from_left(from_right(pair, 0), 0)

    def inverse(pair):
        return from_right(from_left(pair, 1), 1)

    def both(ref, first):
        return tuple((ref[first + i, 0], ref[first + i, 1]) for i in (0, 1))

    def keep(ref, first, pair):
        for i in (0, 1):
            ref[first + i, 0] = pair[i][0]
            ref[first + i, 1] = pair[i][1]

    def add_gradient(s, first, pair):
        chosen = [masks(first + i) for i in (0, 1)]
        for part in (0, 1):
            for a in (0, 1):
                for b in (0, 1):
                    total = grad[s, a, b, part]
                    for i in (0, 1):
                        in_rows, in_cols = chosen[i]
                        in_rows = jnp.logical_not(in_rows) if a else in_rows
                        in_cols = jnp.logical_not(in_cols) if b else in_cols
                        total = total + jnp.where(in_rows & in_cols, pair[i][part], 0.0)
                    grad[s, a, b, part] = total

    def to_inner(first):
        entry = tuple(
            times((shifted[first + i, 0], shifted[first + i, 1]), window(0, first + i))
            for i in (0, 1)
        )
        propagator = (prop[0], prop[1])
        spec = tuple(times(propagator, x) for x in forward(entry))
        keep(inner, first, inverse(spec))

    def to_back(first):
        second = tuple(window(1, first + i) for i in (0, 1))
        far = forward(tuple(times(x, o) for x, o in zip(both(inner, first), second)))
        scaled = []
        for i in (0, 1):
            re, im = far[i]
            misfit = re * re + im * im - meas_ref[first + i]
            scaled.append((misfit * re, misfit * im))
        back = inverse(tuple(scaled))
        keep(wave, first, tuple(conj_times(o, x) for o, x in zip(second, back)))
        add_gradient(
            1, first, tuple(conj_times(x, y) for x, y in zip(both(inner, first), back))
        )

    def to_first(first):
        propagator = (prop[0], prop[1])
        spec = tuple(conj_times(propagator, x) for x in forward(both(wave, first)))
        out = inverse(spec)
        add_gradient(
            0, first, tuple(conj_times(p, x) for p, x in zip(both(shifted, first), out))
        )

    grad[...] = jnp.zeros_like(grad)
    arrive(IN_VC, 0)
    arrive(IN_VH, 0)

    @pl.loop(0, count // 2)
    def _(i):
        to_inner(2 * i)

    arrive(IN_VC, 1)
    arrive(IN_VH, 1)

    @pl.loop(0, count // 2)
    def _(i):
        to_back(2 * i)

    def after_gv(s):
        arrive(G_V, s)
        send_gh[s, HIGH], send_gh[s, LOW] = pack(
            grad[s, 0, 1, 0] + recv_gv[s, 1, 0], grad[s, 0, 1, 1] + recv_gv[s, 1, 1]
        )
        start(G_H, s)

    def after_gh(s):
        arrive(G_H, s)
        moved = joined(recv_gh[s, HIGH], recv_gh[s, LOW])
        for part in (0, 1):
            total = grad[s, 0, 0, part] + recv_gv[s, 0, part] + moved[part]
            grad[s, 0, 0, part] = obj_ref[s, part] - step_size * total
        send_uh[s, LOW], send_uh[s, HIGH] = pack(grad[s, 0, 0, 0], grad[s, 0, 0, 1])
        start(U_H, s)

    def own(s):
        return pltpu.make_async_copy(
            ready.at[s], out_ref.at[s, :, pl.ds(half, length)], local_sem.at[s]
        )

    def after_uh(s):
        arrive(U_H, s)
        margins = joined(recv_uh[s, LOW], recv_uh[s, HIGH])
        for part in (0, 1):
            center = grad[s, 0, 0, part]
            ready[s, part, :, :length] = swap(jnp.where(low_lanes, center, margins[part]))
            ready[s, part, :, length:] = swap(jnp.where(low_lanes, margins[part], center))
        start(U_V, s)
        own(s).start()

    start(G_V, 1)
    to_first(0)
    after_gv(1)
    if count > 2:
        to_first(2)
    after_gh(1)
    for first in range(4, count, 2):
        to_first(first)
    start(G_V, 0)
    after_uh(1)
    after_gv(0)
    after_gh(0)
    after_uh(0)
    for s in (0, 1):
        arrive(U_V, s)
        own(s).wait()
    for way in (LOW, HIGH):
        @pl.when(jnp.logical_not(exists[0][way]))
        def _():
            place = pl.ds(0, half) if way == LOW else pl.ds(half + length, half)
            pltpu.make_async_copy(zero, out_ref.at[:, :, place], edge_sem.at[way]).wait()
    for kind in range(7):
        for s in (0, 1):
            leave(kind, s)


def per_device(rows, cols, object_tiles, positions, probe, phase, intensity):
    length = probe.shape[1]
    count = positions.shape[2]
    half = length // 2
    tables = jnp.asarray(dft_tables(length))
    vmem = pl.BlockSpec(memory_space=pltpu.VMEM)
    f32 = jnp.float32
    sq = (length, length)
    scratch = [
        (2, 2) + sq,
        (2, 2) + sq,
        (2, 2) + sq,
        (2, 2) + sq,
        (2, 2) + sq,
        (count, 2) + sq,
        (2,) + sq,
        (count, 2) + sq,
        (count, 2) + sq,
        (2, 2, 2, 2) + sq,
        (2, 2, 2) + sq,
        (2, 2) + sq,
        (2, 2) + sq,
        (2, 2) + sq,
        (2, 2) + sq,
        (2, 2, length, 2 * length),
        (2, 2, half, 2 * length),
    ]
    return pl.pallas_call(
        functools.partial(kernel, rows, cols),
        out_shape=jax.ShapeDtypeStruct((2, 2, 2 * length, 2 * length), f32),
        in_specs=[pl.BlockSpec(memory_space=pltpu.SMEM)] + [vmem] * 5,
        out_specs=pl.BlockSpec(memory_space=pl.ANY),
        scratch_shapes=[pltpu.VMEM(shape, f32) for shape in scratch]
        + [
            pltpu.SemaphoreType.DMA((7, 2, 2)),
            pltpu.SemaphoreType.DMA((7, 2, 2)),
            pltpu.SemaphoreType.DMA((2,)),
            pltpu.SemaphoreType.DMA((2,)),
        ],
        compiler_params=pltpu.CompilerParams(
            collective_id=0, has_side_effects=True, vmem_limit_bytes=40 * 1024 * 1024
        ),
    )(positions[0, 0], object_tiles, probe, phase, intensity[0, 0], tables)


def solution(mesh):
    return jax.shard_map(
        functools.partial(per_device, mesh.shape["row"], mesh.shape["col"]),
        mesh=mesh,
        in_specs=(
            P(None, None, "row", "col"),
            P("row", "col", None, None),
            P(),
            P(),
            P("row", "col", None, None, None),
        ),
        out_specs=P(None, None, "row", "col"),
        check_vma=False,
    )
```

profile of v0, /device:TPU:5, one launch (start us, length us, event | category | flops | bytes accessed | tf_op | source)
XLA Modules:
  0.0 54.0 jit_solution(626355349879408103)
XLA Ops:
  0.0 0.0 copy-start.5
  0.0 0.7 %copy-done.5 = s32[1,1,6,2]{2,3,1,0:T(2,128)S(1)} copy-done((s32[1,1,6,2]{2,3,1,0:T(2,128)S(1)}, s32[1,1,6,2]{2,3,1,0:T(2,128)}, u32[]{:S(2)}) %copy-start.5) | copy-done | bytes 72
  0.7 0.1 copy.7.pos_ref
  0.8 0.0 copy-start
  0.8 1.0 %copy-done = bf16[2,2,256,256]{3,2,1,0:T(8,128)(2,1)S(1)} copy-done((bf16[2,2,256,256]{3,2,1,0:T(8,128)(2,1)S(1)}, bf16[2,2,256,256]{3,2,1,0:T(8,128)(2,1)}, u32[]{:S(2)}) %copy-start) | copy-done | bytes 524312
  1.8 0.0 copy-start.1
  1.8 1.0 %copy-done.1 = f32[1,1,6,128,128]{4,3,2,1,0:T(8,128)S(1)} copy-done((f32[1,1,6,128,128]{4,3,2,1,0:T(8,128)S(1)}, f32[1,1,6,128,128]{4,3,2,1,0:T(8,128)}, u32[]{:S(2)}) %copy-start.1) | copy-done | bytes 393240
  2.8 0.0 copy-start.2
  2.8 0.9 %copy-done.2 = f32[2,2,128,128]{3,2,1,0:T(8,128)S(1)} copy-done((f32[2,2,128,128]{3,2,1,0:T(8,128)S(1)}, f32[2,2,128,128]{3,2,1,0:T(8,128)}, u32[]{:S(2)}) %copy-start.2) | copy-done | bytes 262168
  3.8 0.0 copy-start.3
  3.8 0.9 %copy-done.3 = f32[2,128,128]{2,1,0:T(8,128)S(1)} copy-done((f32[2,128,128]{2,1,0:T(8,128)S(1)}, f32[2,128,128]{2,1,0:T(8,128)}, u32[]{:S(2)}) %copy-start.3) | copy-done | bytes 131096
  4.7 0.0 copy-start.4
  4.7 0.8 %copy-done.4 = f32[128,128]{1,0:T(8,128)S(1)} copy-done((f32[128,128]{1,0:T(8,128)S(1)}, f32[128,128]{1,0:T(8,128)}, u32[]{:S(2)}) %copy-start.4) | copy-done | bytes 65560
  5.5 47.6 %shard_map.64 = f32[2,2,256,256]{3,2,1,0:T(8,128)S(1)} custom-call(s32[6,2]{1,0:T(8,128)S(1)} %copy.7.pos_ref, f32[2,2,128,128]{3,2,1,0:T(8,128)S(1)} %copy-done.2, f32[2,128,128]{2,1,0:T(8,128)S(1)} %copy-done.3, f32[128,128]{1,0:T(8,128)S(1)} %copy-done.4, f32[6,128,128]{2,1,0:T(8,128)S(1)} %bitcast.2, bf16[2,2,256,256]{3,2,1,0:T(8,128)(2,1)S(1)} %copy-done), custom_call_target="tpu_custom_call" | custom-call | tf_op jit(solution)/shard_map/pallas_call | solution.py:373
  53.1 1.0 %copy.9 = f32[2,2,256,256]{3,2,1,0:T(8,128)} copy(f32[2,2,256,256]{3,2,1,0:T(8,128)S(1)} %shard_map.64) | data formatting | bytes 2097152
Async XLA Ops:
  0.0 0.7 %copy-start.5 = (s32[1,1,6,2]{2,3,1,0:T(2,128)S(1)}, s32[1,1,6,2]{2,3,1,0:T(2,128)}, u32[]{:S(2)}) copy-start(s32[1,1,6,2]{2,3,1,0:T(2,128)} %param.7) | copy-start | bytes 148
  0.8 1.0 %copy-start = (bf16[2,2,256,256]{3,2,1,0:T(8,128)(2,1)S(1)}, bf16[2,2,256,256]{3,2,1,0:T(8,128)(2,1)}, u32[]{:S(2)}) copy-start(bf16[2,2,256,256]{3,2,1,0:T(8,128)(2,1)} %constant.2.clone.table_ref) | copy-start | bytes 1572868
  1.8 1.0 %copy-start.1 = (f32[1,1,6,128,128]{4,3,2,1,0:T(8,128)S(1)}, f32[1,1,6,128,128]{4,3,2,1,0:T(8,128)}, u32[]{:S(2)}) copy-start(f32[1,1,6,128,128]{4,3,2,1,0:T(8,128)} %param.10) | copy-start | bytes 1179652
  2.8 0.9 %copy-start.2 = (f32[2,2,128,128]{3,2,1,0:T(8,128)S(1)}, f32[2,2,128,128]{3,2,1,0:T(8,128)}, u32[]{:S(2)}) copy-start(f32[2,2,128,128]{3,2,1,0:T(8,128)} %obj_ref.1) | copy-start | bytes 786436
  3.8 0.9 %copy-start.3 = (f32[2,128,128]{2,1,0:T(8,128)S(1)}, f32[2,128,128]{2,1,0:T(8,128)}, u32[]{:S(2)}) copy-start(f32[2,128,128]{2,1,0:T(8,128)} %probe_ref.1) | copy-start | bytes 393220
  4.7 0.8 %copy-start.4 = (f32[128,128]{1,0:T(8,128)S(1)}, f32[128,128]{1,0:T(8,128)}, u32[]{:S(2)}) copy-start(f32[128,128]{1,0:T(8,128)} %phase_ref.1) | copy-start | bytes 196612
where the time goes:
time: 54.4 us; the launch traced here: 54 us
  Pallas kernels  47.6 us (88%)
  local copies, waits for them, and re-layouts  6.47 us (12%)
    pallas_call x1, Pallas kernels, per_device(): pl.pallas_call(functools.partial(kernel, rows, cols), out_shape=jax.Shape...  47.6 us
    unnamed x13, local copies, waits for them, and re-layouts  6.38 us

commit v1 on v0

--- a/solution.py
+++ b/solution.py
@@ -12,7 +12,7 @@
 
 step_size = 2.0
 MESH = pl.DeviceIdType.MESH
-IN_H, IN_VC, IN_VH, G_V, G_H, U_H, U_V = range(7)
+IN_H, IN_VC, IN_VH, G_V, G_H, U_V = range(6)
 LOW, HIGH = 0, 1
 
 
@@ -47,14 +47,14 @@
 
 
 def kernel(
-    rows, cols, pos_ref, obj_ref, probe_ref, phase_ref, meas_ref, table_ref, out_ref,
-    send_h, recv_h, side, vert_c, vert_h, shifted, prop, inner, wave,
-    grad, recv_gv, send_gh, recv_gh, send_uh, recv_uh, ready, zero,
-    send_sem, recv_sem, local_sem, edge_sem,
+    rows, cols, pos_ref, obj_hbm, probe_hbm, phase_hbm, meas_hbm, table_hbm, out_ref,
+    obj_ref, probe_ref, phase_ref, meas_ref, table_ref, send_h, recv_h, side, vert_c, vert_h, shifted, prop, inner, wave,
+    grad, recv_gv, send_gh, recv_gh, ready, zero,
+    send_sem, recv_sem, local_sem, edge_sem, load_sem,
 ):
     length = probe_ref.shape[1]
     half = length // 2
-    count = pos_ref.shape[0]
+    count = pos_ref.shape[1]
     row, col = lax.axis_index("row"), lax.axis_index("col")
     lane = lax.broadcasted_iota(jnp.int32, (length, length), 1)
     line = lax.broadcasted_iota(jnp.int32, (length, length), 0)
@@ -78,7 +78,7 @@
         )
 
     def remote(kind, s, way, source, target):
-        axis = 1 if kind in (IN_H, G_H, U_H) else 0
+        axis = 1 if kind in (IN_H, G_H) else 0
         return pltpu.make_async_remote_copy(
             src_ref=source, dst_ref=target,
             send_sem=send_sem.at[kind, s, way], recv_sem=recv_sem.at[kind, s, way],
@@ -99,15 +99,13 @@
             pair = grad.at[s, 1, :, :, other], recv_gv.at[s, :, :, other]
         elif kind == G_H:
             pair = send_gh.at[s, way], recv_gh.at[s, way]
-        elif kind == U_H:
-            pair = send_uh.at[s, way], recv_uh.at[s, way]
         else:
             place = pl.ds(half + length, half) if way == LOW else pl.ds(0, half)
             pair = ready.at[s, :, part], out_ref.at[s, :, place]
         return remote(kind, s, way, *pair)
 
     def axis_of(kind):
-        return 1 if kind in (IN_H, G_H, U_H) else 0
+        return 1 if kind in (IN_H, G_H) else 0
 
     def start(kind, s):
         for way in (LOW, HIGH):
@@ -127,9 +125,24 @@
             def _():
                 copies(kind, s, way).wait_send()
 
+    loads = [
+        pltpu.make_async_copy(source, target, load_sem.at[i])
+        for i, (source, target) in enumerate(
+            (
+                (obj_hbm, obj_ref),
+                (probe_hbm, probe_ref),
+                (phase_hbm, phase_ref),
+                (table_hbm, table_ref),
+                (meas_hbm.at[0, 0], meas_ref),
+            )
+        )
+    ]
+    for load in loads:
+        load.start()
+
+    recv_h[...] = jnp.zeros_like(recv_h)
     recv_gv[...] = jnp.zeros_like(recv_gv)
     recv_gh[...] = jnp.zeros_like(recv_gh)
-    recv_uh[...] = jnp.zeros_like(recv_uh)
     zero[...] = jnp.zeros_like(zero)
 
     barrier = pltpu.get_barrier_semaphore()
@@ -138,6 +151,7 @@
             @pl.when(exists[axis][way])
             def _():
                 pl.semaphore_signal(barrier, inc=1, device_id=places[axis][way], device_id_type=MESH)
+    loads[0].wait()
     for s in (0, 1):
         send_h[s, LOW], send_h[s, HIGH] = pack(obj_ref[s, 0], obj_ref[s, 1])
     peers = sum(there.astype(jnp.int32) for pair in exists for there in pair)
@@ -154,22 +168,28 @@
             place = pl.ds(0, half) if way == LOW else pl.ds(half + length, half)
             pltpu.make_async_copy(zero, out_ref.at[:, :, place], edge_sem.at[way]).start()
 
+    loads[1].wait()
     for number in range(count):
-        down = (pos_ref[number, 0] + half) % length
-        across = (pos_ref[number, 1] + half) % length
+        down = (pos_ref[0, number] + half) % length
+        across = (pos_ref[1, number] + half) % length
         for part in (0, 1):
             moved = pltpu.roll(probe_ref[part], down, 0)
             shifted[number, part] = pltpu.roll(moved, across, 1)
+    loads[2].wait()
     prop[0] = jnp.cos(phase_ref[...])
     prop[1] = jnp.sin(phase_ref[...])
 
-    for s in (0, 1):
+    grad[...] = jnp.zeros_like(grad)
+
+    def after_h(s):
         arrive(IN_H, s)
         side[s, 0], side[s, 1] = joined(recv_h[s, LOW], recv_h[s, HIGH])
         start(IN_VH, s)
 
+    after_h(0)
+
     def masks(number):
-        down, across = pos_ref[number, 0] - half, pos_ref[number, 1] - half
+        down, across = pos_ref[0, number] - half, pos_ref[1, number] - half
         in_rows = (line >= down) & (line < down + length)
         in_cols = (lane >= across) & (lane < across + length)
         return in_rows, in_cols
@@ -271,65 +291,57 @@
             0, first, tuple(conj_times(p, x) for p, x in zip(both(shifted, first), out))
         )
 
-    grad[...] = jnp.zeros_like(grad)
+    loads[3].wait()
+    loads[4].wait()
     arrive(IN_VC, 0)
     arrive(IN_VH, 0)
-
-    @pl.loop(0, count // 2)
-    def _(i):
-        to_inner(2 * i)
-
+    for first in range(0, count, 2):
+        to_inner(first)
+        if first == 0:
+            after_h(1)
     arrive(IN_VC, 1)
     arrive(IN_VH, 1)
-
-    @pl.loop(0, count // 2)
-    def _(i):
-        to_back(2 * i)
+    for first in range(0, count, 2):
+        to_back(first)
 
     def after_gv(s):
         arrive(G_V, s)
-        send_gh[s, HIGH], send_gh[s, LOW] = pack(
-            grad[s, 0, 1, 0] + recv_gv[s, 1, 0], grad[s, 0, 1, 1] + recv_gv[s, 1, 1]
-        )
+        for part in (0, 1):
+            center = grad[s, 0, 0, part] + recv_gv[s, 0, part]
+            margin = grad[s, 0, 1, part] + recv_gv[s, 1, part]
+            grad[s, 0, 0, part] = center
+            grad[s, 0, 1, part] = margin
+            send_gh[s, HIGH, part] = jnp.where(low_lanes, margin, center)
+            send_gh[s, LOW, part] = jnp.where(low_lanes, center, margin)
         start(G_H, s)
-
-    def after_gh(s):
-        arrive(G_H, s)
-        moved = joined(recv_gh[s, HIGH], recv_gh[s, LOW])
-        for part in (0, 1):
-            total = grad[s, 0, 0, part] + recv_gv[s, 0, part] + moved[part]
-            grad[s, 0, 0, part] = obj_ref[s, part] - step_size * total
-        send_uh[s, LOW], send_uh[s, HIGH] = pack(grad[s, 0, 0, 0], grad[s, 0, 0, 1])
-        start(U_H, s)
 
     def own(s):
         return pltpu.make_async_copy(
             ready.at[s], out_ref.at[s, :, pl.ds(half, length)], local_sem.at[s]
         )
 
-    def after_uh(s):
-        arrive(U_H, s)
-        margins = joined(recv_uh[s, LOW], recv_uh[s, HIGH])
+    def after_gh(s):
+        arrive(G_H, s)
         for part in (0, 1):
-            center = grad[s, 0, 0, part]
-            ready[s, part, :, :length] = swap(jnp.where(low_lanes, center, margins[part]))
-            ready[s, part, :, length:] = swap(jnp.where(low_lanes, margins[part], center))
+            from_left, from_right = recv_gh[s, HIGH, part], recv_gh[s, LOW, part]
+            center = grad[s, 0, 0, part] + jnp.where(low_lanes, from_left, from_right)
+            margin = grad[s, 0, 1, part] + jnp.where(low_lanes, from_right, from_left)
+            center = obj_ref[s, part] - step_size * center
+            margin = side[s, part] - step_size * margin
+            ready[s, part, :, :length] = swap(jnp.where(low_lanes, center, margin))
+            ready[s, part, :, length:] = swap(jnp.where(low_lanes, margin, center))
         start(U_V, s)
         own(s).start()
 
     start(G_V, 1)
-    to_first(0)
-    after_gv(1)
-    if count > 2:
-        to_first(2)
-    after_gh(1)
-    for first in range(4, count, 2):
+    for first in range(0, count, 2):
+        if first == count - 2:
+            after_gv(1)
         to_first(first)
     start(G_V, 0)
-    after_uh(1)
+    after_gh(1)
     after_gv(0)
     after_gh(0)
-    after_uh(0)
     for s in (0, 1):
         arrive(U_V, s)
         own(s).wait()
@@ -338,7 +350,7 @@
         def _():
             place = pl.ds(0, half) if way == LOW else pl.ds(half + length, half)
             pltpu.make_async_copy(zero, out_ref.at[:, :, place], edge_sem.at[way]).wait()
-    for kind in range(7):
+    for kind in range(6):
         for s in (0, 1):
             leave(kind, s)
 
@@ -348,10 +360,15 @@
     count = positions.shape[2]
     half = length // 2
     tables = jnp.asarray(dft_tables(length))
-    vmem = pl.BlockSpec(memory_space=pltpu.VMEM)
+    anywhere = pl.BlockSpec(memory_space=pl.ANY)
     f32 = jnp.float32
     sq = (length, length)
     scratch = [
+        object_tiles.shape,
+        probe.shape,
+        phase.shape,
+        intensity.shape[2:],
+        None,
         (2, 2) + sq,
         (2, 2) + sq,
         (2, 2) + sq,
@@ -363,29 +380,31 @@
         (count, 2) + sq,
         (2, 2, 2, 2) + sq,
         (2, 2, 2) + sq,
-        (2, 2) + sq,
-        (2, 2) + sq,
-        (2, 2) + sq,
-        (2, 2) + sq,
+        (2, 2, 2) + sq,
+        (2, 2, 2) + sq,
         (2, 2, length, 2 * length),
         (2, 2, half, 2 * length),
     ]
     return pl.pallas_call(
         functools.partial(kernel, rows, cols),
         out_shape=jax.ShapeDtypeStruct((2, 2, 2 * length, 2 * length), f32),
-        in_specs=[pl.BlockSpec(memory_space=pltpu.SMEM)] + [vmem] * 5,
+        in_specs=[pl.BlockSpec(memory_space=pltpu.SMEM)] + [anywhere] * 5,
         out_specs=pl.BlockSpec(memory_space=pl.ANY),
-        scratch_shapes=[pltpu.VMEM(shape, f32) for shape in scratch]
+        scratch_shapes=[
+            pltpu.VMEM(shape, f32) if shape else pltpu.VMEM(tables.shape, tables.dtype)
+            for shape in scratch
+        ]
         + [
-            pltpu.SemaphoreType.DMA((7, 2, 2)),
-            pltpu.SemaphoreType.DMA((7, 2, 2)),
+            pltpu.SemaphoreType.DMA((6, 2, 2)),
+            pltpu.SemaphoreType.DMA((6, 2, 2)),
             pltpu.SemaphoreType.DMA((2,)),
             pltpu.SemaphoreType.DMA((2,)),
+            pltpu.SemaphoreType.DMA((5,)),
         ],
         compiler_params=pltpu.CompilerParams(
-            collective_id=0, has_side_effects=True, vmem_limit_bytes=40 * 1024 * 1024
+            collective_id=0, has_side_effects=True, vmem_limit_bytes=60 * 1024 * 1024
         ),
-    )(positions[0, 0], object_tiles, probe, phase, intensity[0, 0], tables)
+    )(positions[0, 0].T, object_tiles, probe, phase, intensity, tables)
 
 
 def solution(mesh):

time: 54.4 us -> 44.2 us (0.81)
  Pallas kernels: 47.6 us -> 41.7 us
  local copies, waits for them, and re-layouts: 6.47 us -> 2.29 us
    pallas_call x1, Pallas kernels: 47.6 us -> 41.7 us  [per_device(): pl.pallas_call(functools.partial(kernel, rows, cols), out_shape=jax.Shape...]
    unnamed x13 -> x1, local copies, waits for them, and re-layouts: 6.38 us -> 2.29 us
where the time goes in v1:
time: 44.2 us; the launch traced here: 44 us
  Pallas kernels  41.7 us (94%)
  local copies, waits for them, and re-layouts  2.29 us (5%)
    pallas_call x1, Pallas kernels, per_device(): pl.pallas_call(functools.partial(kernel, rows, cols), out_shape=jax.Shape...  41.7 us
    unnamed x1, local copies, waits for them, and re-layouts  2.29 us

profile of v1, /device:TPU:5, one launch (start us, length us, event | category | flops | bytes accessed | tf_op | source)
XLA Modules:
  0.0 44.0 jit_solution(8568427481048997421)
XLA Ops:
  0.0 41.7 %shard_map.64 = f32[2,2,256,256]{3,2,1,0:T(8,128)} custom-call(s32[2,6]{1,0:T(2,128)} %bitcast.3, f32[2,2,128,128]{3,2,1,0:T(8,128)} %obj_hbm.1, f32[2,128,128]{2,1,0:T(8,128)} %probe_hbm.1, f32[128,128]{1,0:T(8,128)} %phase_hbm.1, f32[1,1,6,128,128]{4,3,2,1,0:T(8,128)} %meas_hbm.1, bf16[2,2,256,256]{3,2,1,0:T(8,128)(2,1)} %constant.2.clone.table_hbm), custom_call_target="tpu_custom_call" | custom-call | tf_op jit(solution)/shard_map/pallas_call | solution.py:388
  41.7 2.3 %copy.8 = f32[2,2,256,256]{3,2,1,0:T(8,128)} copy(f32[2,2,256,256]{3,2,1,0:T(8,128)} %shard_map.64) | data formatting | bytes 2097152

commit v2 on v1

--- a/solution.py
+++ b/solution.py
@@ -77,53 +77,53 @@
             jnp.where(low_lanes, swap(low_pack), high_pack),
         )
 
-    def remote(kind, s, way, source, target):
+    def remote(kind, s, part, way, source, target):
         axis = 1 if kind in (IN_H, G_H) else 0
         return pltpu.make_async_remote_copy(
             src_ref=source, dst_ref=target,
-            send_sem=send_sem.at[kind, s, way], recv_sem=recv_sem.at[kind, s, way],
+            send_sem=send_sem.at[kind, s, part, way], recv_sem=recv_sem.at[kind, s, part, way],
             device_id=places[axis][way], device_id_type=MESH,
         )
 
-    def copies(kind, s, way):
+    def copies(kind, s, part, way):
         top, bottom = pl.ds(0, half), pl.ds(half, half)
-        part = top if way == LOW else bottom
-        other = bottom if way == LOW else top
+        near = top if way == LOW else bottom
+        far = bottom if way == LOW else top
         if kind == IN_H:
             pair = send_h.at[s, way], recv_h.at[s, way]
         elif kind == IN_VC:
-            pair = obj_ref.at[s, :, part], vert_c.at[s, :, part]
+            pair = obj_ref.at[s, :, near], vert_c.at[s, :, near]
         elif kind == IN_VH:
-            pair = side.at[s, :, part], vert_h.at[s, :, part]
+            pair = side.at[s, :, near], vert_h.at[s, :, near]
         elif kind == G_V:
-            pair = grad.at[s, 1, :, :, other], recv_gv.at[s, :, :, other]
+            pair = grad.at[s, 1, :, part, far], recv_gv.at[s, :, part, far]
         elif kind == G_H:
-            pair = send_gh.at[s, way], recv_gh.at[s, way]
+            pair = send_gh.at[s, way, part], recv_gh.at[s, way, part]
         else:
             place = pl.ds(half + length, half) if way == LOW else pl.ds(0, half)
-            pair = ready.at[s, :, part], out_ref.at[s, :, place]
-        return remote(kind, s, way, *pair)
+            pair = ready.at[s, part, near], out_ref.at[s, part, place]
+        return remote(kind, s, part, way, *pair)
 
     def axis_of(kind):
         return 1 if kind in (IN_H, G_H) else 0
 
-    def start(kind, s):
+    def start(kind, s, part=0):
         for way in (LOW, HIGH):
             @pl.when(exists[axis_of(kind)][way])
             def _():
-                copies(kind, s, way).start()
-
-    def arrive(kind, s):
+                copies(kind, s, part, way).start()
+
+    def arrive(kind, s, part=0):
         for way in (LOW, HIGH):
             @pl.when(exists[axis_of(kind)][1 - way])
             def _():
-                copies(kind, s, way).wait_recv()
-
-    def leave(kind, s):
+                copies(kind, s, part, way).wait_recv()
+
+    def leave(kind, s, part=0):
         for way in (LOW, HIGH):
             @pl.when(exists[axis_of(kind)][way])
             def _():
-                copies(kind, s, way).wait_send()
+                copies(kind, s, part, way).wait_send()
 
     loads = [
         pltpu.make_async_copy(source, target, load_sem.at[i])
@@ -159,8 +159,6 @@
 
     start(IN_H, 0)
     start(IN_VC, 0)
-    start(IN_H, 1)
-    start(IN_VC, 1)
 
     for way in (LOW, HIGH):
         @pl.when(jnp.logical_not(exists[0][way]))
@@ -175,6 +173,10 @@
         for part in (0, 1):
             moved = pltpu.roll(probe_ref[part], down, 0)
             shifted[number, part] = pltpu.roll(moved, across, 1)
+    leave(IN_H, 0)
+    start(IN_H, 1)
+    start(IN_VC, 1)
+
     loads[2].wait()
     prop[0] = jnp.cos(phase_ref[...])
     prop[1] = jnp.sin(phase_ref[...])
@@ -304,55 +306,60 @@
     for first in range(0, count, 2):
         to_back(first)
 
-    def after_gv(s):
-        arrive(G_V, s)
-        for part in (0, 1):
-            center = grad[s, 0, 0, part] + recv_gv[s, 0, part]
-            margin = grad[s, 0, 1, part] + recv_gv[s, 1, part]
-            grad[s, 0, 0, part] = center
-            grad[s, 0, 1, part] = margin
-            send_gh[s, HIGH, part] = jnp.where(low_lanes, margin, center)
-            send_gh[s, LOW, part] = jnp.where(low_lanes, center, margin)
-        start(G_H, s)
-
-    def own(s):
+    def after_gv(s, part):
+        arrive(G_V, s, part)
+        center = grad[s, 0, 0, part] + recv_gv[s, 0, part]
+        margin = grad[s, 0, 1, part] + recv_gv[s, 1, part]
+        send_gh[s, HIGH, part] = jnp.where(low_lanes, margin, center)
+        send_gh[s, LOW, part] = jnp.where(low_lanes, center, margin)
+        start(G_H, s, part)
+        grad[s, 0, 0, part] = obj_ref[s, part] - step_size * center
+        grad[s, 0, 1, part] = side[s, part] - step_size * margin
+
+    def own(s, part):
         return pltpu.make_async_copy(
-            ready.at[s], out_ref.at[s, :, pl.ds(half, length)], local_sem.at[s]
-        )
-
-    def after_gh(s):
-        arrive(G_H, s)
-        for part in (0, 1):
-            from_left, from_right = recv_gh[s, HIGH, part], recv_gh[s, LOW, part]
-            center = grad[s, 0, 0, part] + jnp.where(low_lanes, from_left, from_right)
-            margin = grad[s, 0, 1, part] + jnp.where(low_lanes, from_right, from_left)
-            center = obj_ref[s, part] - step_size * center
-            margin = side[s, part] - step_size * margin
-            ready[s, part, :, :length] = swap(jnp.where(low_lanes, center, margin))
-            ready[s, part, :, length:] = swap(jnp.where(low_lanes, margin, center))
-        start(U_V, s)
-        own(s).start()
-
-    start(G_V, 1)
+            ready.at[s, part], out_ref.at[s, part, pl.ds(half, length)], local_sem.at[s, part]
+        )
+
+    def after_gh(s, part):
+        arrive(G_H, s, part)
+        from_left, from_right = recv_gh[s, HIGH, part], recv_gh[s, LOW, part]
+        center = grad[s, 0, 0, part] - step_size * jnp.where(low_lanes, from_left, from_right)
+        margin = grad[s, 0, 1, part] - step_size * jnp.where(low_lanes, from_right, from_left)
+        ready[s, part, :, :length] = swap(jnp.where(low_lanes, center, margin))
+        ready[s, part, :, length:] = swap(jnp.where(low_lanes, margin, center))
+        start(U_V, s, part)
+        own(s, part).start()
+
+    start(G_V, 1, 0)
+    start(G_V, 1, 1)
     for first in range(0, count, 2):
-        if first == count - 2:
-            after_gv(1)
         to_first(first)
-    start(G_V, 0)
-    after_gh(1)
-    after_gv(0)
-    after_gh(0)
+    start(G_V, 0, 0)
+    start(G_V, 0, 1)
+    for s in (1, 0):
+        for part in (0, 1):
+            after_gv(s, part)
+    for s in (1, 0):
+        for part in (0, 1):
+            after_gh(s, part)
     for s in (0, 1):
-        arrive(U_V, s)
-        own(s).wait()
+        for part in (0, 1):
+            arrive(U_V, s, part)
+            own(s, part).wait()
     for way in (LOW, HIGH):
         @pl.when(jnp.logical_not(exists[0][way]))
         def _():
             place = pl.ds(0, half) if way == LOW else pl.ds(half + length, half)
             pltpu.make_async_copy(zero, out_ref.at[:, :, place], edge_sem.at[way]).wait()
-    for kind in range(6):
-        for s in (0, 1):
-            leave(kind, s)
+    leave(IN_H, 1)
+    for s in (0, 1):
+        leave(IN_VC, s)
+        leave(IN_VH, s)
+        for part in (0, 1):
+            leave(G_V, s, part)
+            leave(G_H, s, part)
+            leave(U_V, s, part)
 
 
 def per_device(rows, cols, object_tiles, positions, probe, phase, intensity):
@@ -395,9 +402,9 @@
             for shape in scratch
         ]
         + [
-            pltpu.SemaphoreType.DMA((6, 2, 2)),
-            pltpu.SemaphoreType.DMA((6, 2, 2)),
-            pltpu.SemaphoreType.DMA((2,)),
+            pltpu.SemaphoreType.DMA((6, 2, 2, 2)),
+            pltpu.SemaphoreType.DMA((6, 2, 2, 2)),
+            pltpu.SemaphoreType.DMA((2, 2)),
             pltpu.SemaphoreType.DMA((2,)),
             pltpu.SemaphoreType.DMA((5,)),
         ],

time: 44.2 us -> 40.4 us (0.914)
  Pallas kernels: 41.7 us -> 37.7 us
    pallas_call x1, Pallas kernels: 41.7 us -> 37.7 us  [per_device(): pl.pallas_call(functools.partial(kernel, rows, cols), out_shape=jax.Shape...]
where the time goes in v2:
time: 40.4 us; the launch traced here: 40 us
  Pallas kernels  37.7 us (93%)
  local copies, waits for them, and re-layouts  2.29 us (6%)
    pallas_call x1, Pallas kernels, per_device(): pl.pallas_call(functools.partial(kernel, rows, cols), out_shape=jax.Shape...  37.7 us
    unnamed x1, local copies, waits for them, and re-layouts  2.29 us

profile of v2, /device:TPU:5, one launch (start us, length us, event | category | flops | bytes accessed | tf_op | source)
XLA Modules:
  0.0 40.0 jit_solution(1544243138369015534)
XLA Ops:
  0.0 37.7 %shard_map.64 = f32[2,2,256,256]{3,2,1,0:T(8,128)} custom-call(s32[2,6]{1,0:T(2,128)} %bitcast.3, f32[2,2,128,128]{3,2,1,0:T(8,128)} %obj_hbm.1, f32[2,128,128]{2,1,0:T(8,128)} %probe_hbm.1, f32[128,128]{1,0:T(8,128)} %phase_hbm.1, f32[1,1,6,128,128]{4,3,2,1,0:T(8,128)} %meas_hbm.1, bf16[2,2,256,256]{3,2,1,0:T(8,128)(2,1)} %constant.2.clone.table_hbm), custom_call_target="tpu_custom_call" | custom-call | tf_op jit(solution)/shard_map/pallas_call | solution.py:395
  37.7 2.3 %copy.8 = f32[2,2,256,256]{3,2,1,0:T(8,128)} copy(f32[2,2,256,256]{3,2,1,0:T(8,128)} %shard_map.64) | data formatting | bytes 2097152

commit v3 on v2

--- a/solution.py
+++ b/solution.py
@@ -207,33 +207,40 @@
             for part in (0, 1)
         )
 
-    def from_right(pair, way):
-        (a_re, a_im), (b_re, b_im) = pair
+    def from_right(pairs, way):
         high, low = split(
             jnp.concatenate(
-                [jnp.concatenate([a_re, a_im], 1), jnp.concatenate([b_re, b_im], 1)], 0
-            )
-        )
-        th, tl = table_ref[way, 0], table_ref[way, 1]
-        y = dot(high, th) + dot(low, th) + dot(high, tl)
-        return (
-            (y[:length, :length], y[:length, length:]),
-            (y[length:, :length], y[length:, length:]),
-        )
-
-    def from_left(pair, way):
-        (a_re, a_im), (b_re, b_im) = pair
-        high, low = split(
-            jnp.concatenate(
-                [jnp.concatenate([a_re, b_re], 1), jnp.concatenate([a_im, b_im], 1)], 0
-            )
-        )
+                [jnp.concatenate([re, im], 1) for pair in pairs for re, im in pair], 0
+            )
+        )
+        size = high.shape[0]
+        y = dot(jnp.concatenate([high, low], 0), table_ref[way, 0])
+        y = y[:size] + y[size:] + dot(high, table_ref[way, 1])
+        waves = [
+            (y[at : at + length, :length], y[at : at + length, length:])
+            for at in range(0, size, length)
+        ]
+        return [tuple(waves[at : at + 2]) for at in range(0, len(waves), 2)]
+
+    def from_left(pairs, way):
         th, tl = table_ref[1 - way, 0], table_ref[1 - way, 1]
-        y = dot(th, high) + dot(th, low) + dot(tl, high)
-        return (
-            (y[:length, :length], y[length:, :length]),
-            (y[:length, length:], y[length:, length:]),
-        )
+        tables = jnp.concatenate([th, tl], 0)
+        done = []
+        for (a_re, a_im), (b_re, b_im) in pairs:
+            high, low = split(
+                jnp.concatenate(
+                    [jnp.concatenate([a_re, b_re], 1), jnp.concatenate([a_im, b_im], 1)], 0
+                )
+            )
+            y = dot(tables, high)
+            y = y[: 2 * length] + y[2 * length :] + dot(th, low)
+            done.append(
+                (
+                    (y[:length, :length], y[length:, :length]),
+                    (y[:length, length:], y[length:, length:]),
+                )
+            )
+        return done
 
     def forward(pair):
         return from_left(from_right(pair, 0), 0)
@@ -262,49 +269,64 @@
                         total = total + jnp.where(in_rows & in_cols, pair[i][part], 0.0)
                     grad[s, a, b, part] = total
 
-    def to_inner(first):
-        entry = tuple(
-            times((shifted[first + i, 0], shifted[first + i, 1]), window(0, first + i))
-            for i in (0, 1)
-        )
+    pairs_at = range(0, count, 2)
+
+    def to_inner(firsts):
         propagator = (prop[0], prop[1])
-        spec = tuple(times(propagator, x) for x in forward(entry))
-        keep(inner, first, inverse(spec))
-
-    def to_back(first):
-        second = tuple(window(1, first + i) for i in (0, 1))
-        far = forward(tuple(times(x, o) for x, o in zip(both(inner, first), second)))
+        entries = [
+            tuple(
+                times((shifted[first + i, 0], shifted[first + i, 1]), window(0, first + i))
+                for i in (0, 1)
+            )
+            for first in firsts
+        ]
+        specs = [tuple(times(propagator, x) for x in pair) for pair in forward(entries)]
+        for first, pair in zip(firsts, inverse(specs)):
+            keep(inner, first, pair)
+
+    def to_back(firsts):
+        leaving = [
+            tuple(times(x, window(1, first + i)) for i, x in enumerate(both(inner, first)))
+            for first in firsts
+        ]
         scaled = []
-        for i in (0, 1):
-            re, im = far[i]
-            misfit = re * re + im * im - meas_ref[first + i]
-            scaled.append((misfit * re, misfit * im))
-        back = inverse(tuple(scaled))
-        keep(wave, first, tuple(conj_times(o, x) for o, x in zip(second, back)))
-        add_gradient(
-            1, first, tuple(conj_times(x, y) for x, y in zip(both(inner, first), back))
-        )
-
-    def to_first(first):
+        for first, far in zip(firsts, forward(leaving)):
+            waves = []
+            for i in (0, 1):
+                re, im = far[i]
+                misfit = re * re + im * im - meas_ref[first + i]
+                waves.append((misfit * re, misfit * im))
+            scaled.append(tuple(waves))
+        for first, back in zip(firsts, inverse(scaled)):
+            keep(
+                wave, first,
+                tuple(conj_times(window(1, first + i), x) for i, x in enumerate(back)),
+            )
+            add_gradient(
+                1, first, tuple(conj_times(x, y) for x, y in zip(both(inner, first), back))
+            )
+
+    def to_first(firsts):
         propagator = (prop[0], prop[1])
-        spec = tuple(conj_times(propagator, x) for x in forward(both(wave, first)))
-        out = inverse(spec)
-        add_gradient(
-            0, first, tuple(conj_times(p, x) for p, x in zip(both(shifted, first), out))
-        )
+        specs = [
+            tuple(conj_times(propagator, x) for x in pair)
+            for pair in forward([both(wave, first) for first in firsts])
+        ]
+        for first, out in zip(firsts, inverse(specs)):
+            add_gradient(
+                0, first, tuple(conj_times(p, x) for p, x in zip(both(shifted, first), out))
+            )
 
     loads[3].wait()
     loads[4].wait()
     arrive(IN_VC, 0)
     arrive(IN_VH, 0)
-    for first in range(0, count, 2):
-        to_inner(first)
-        if first == 0:
-            after_h(1)
+    to_inner(pairs_at[:1])
+    after_h(1)
+    to_inner(pairs_at[1:])
     arrive(IN_VC, 1)
     arrive(IN_VH, 1)
-    for first in range(0, count, 2):
-        to_back(first)
+    to_back(pairs_at)
 
     def after_gv(s, part):
         arrive(G_V, s, part)
@@ -333,8 +355,7 @@
 
     start(G_V, 1, 0)
     start(G_V, 1, 1)
-    for first in range(0, count, 2):
-        to_first(first)
+    to_first(pairs_at)
     start(G_V, 0, 0)
     start(G_V, 0, 1)
     for s in (1, 0):

time: 40.4 us -> 39.5 us (0.978)
  the two profiles are of different devices: /device:TPU:5 before, /device:TPU:17 now
where the time goes in v3:
time: 39.5 us; the launch traced here: 39.3 us
  Pallas kernels  37 us (94%)
  local copies, waits for them, and re-layouts  2.29 us (6%)
    pallas_call x1, Pallas kernels, per_device(): pl.pallas_call(functools.partial(kernel, rows, cols), out_shape=jax.Shape...  37 us
    unnamed x1, local copies, waits for them, and re-layouts  2.29 us

profile of v3, /device:TPU:17, one launch (start us, length us, event | category | flops | bytes accessed | tf_op | source)
XLA Modules:
  0.0 39.3 jit_solution(14888699393729285484)
XLA Ops:
  0.0 37.0 %shard_map.64 = f32[2,2,256,256]{3,2,1,0:T(8,128)} custom-call(s32[2,6]{1,0:T(2,128)} %bitcast.3, f32[2,2,128,128]{3,2,1,0:T(8,128)} %obj_hbm.1, f32[2,128,128]{2,1,0:T(8,128)} %probe_hbm.1, f32[128,128]{1,0:T(8,128)} %phase_hbm.1, f32[1,1,6,128,128]{4,3,2,1,0:T(8,128)} %meas_hbm.1, bf16[2,2,256,256]{3,2,1,0:T(8,128)(2,1)} %constant.2.clone.table_hbm), custom_call_target="tpu_custom_call" | custom-call | tf_op jit(solution)/shard_map/pallas_call | solution.py:416
  37.0 2.3 %copy.8 = f32[2,2,256,256]{3,2,1,0:T(8,128)} copy(f32[2,2,256,256]{3,2,1,0:T(8,128)} %shard_map.64) | data formatting | bytes 2097152

commit v4 on v3

--- a/solution.py
+++ b/solution.py
@@ -298,19 +298,20 @@
                 waves.append((misfit * re, misfit * im))
             scaled.append(tuple(waves))
         for first, back in zip(firsts, inverse(scaled)):
-            keep(
-                wave, first,
-                tuple(conj_times(window(1, first + i), x) for i, x in enumerate(back)),
-            )
+            keep(wave, first, back)
             add_gradient(
                 1, first, tuple(conj_times(x, y) for x, y in zip(both(inner, first), back))
             )
 
     def to_first(firsts):
         propagator = (prop[0], prop[1])
+        waves = [
+            tuple(conj_times(window(1, first + i), x) for i, x in enumerate(both(wave, first)))
+            for first in firsts
+        ]
         specs = [
             tuple(conj_times(propagator, x) for x in pair)
-            for pair in forward([both(wave, first) for first in firsts])
+            for pair in forward(waves)
         ]
         for first, out in zip(firsts, inverse(specs)):
             add_gradient(
@@ -319,11 +320,10 @@
 
     loads[3].wait()
     loads[4].wait()
+    after_h(1)
     arrive(IN_VC, 0)
     arrive(IN_VH, 0)
-    to_inner(pairs_at[:1])
-    after_h(1)
-    to_inner(pairs_at[1:])
+    to_inner(pairs_at)
     arrive(IN_VC, 1)
     arrive(IN_VH, 1)
     to_back(pairs_at)

time: 39.5 us -> 37.5 us (0.949)
  the two profiles are of different devices: /device:TPU:17 before, /device:TPU:9 now
where the time goes in v4:
time: 37.5 us; the launch traced here: 37.3 us
  Pallas kernels  35.1 us (94%)
  local copies, waits for them, and re-layouts  2.29 us (6%)
    pallas_call x1, Pallas kernels, per_device(): pl.pallas_call(functools.partial(kernel, rows, cols), out_shape=jax.Shape...  35.1 us
    unnamed x1, local copies, waits for them, and re-layouts  2.29 us

profile of v4, /device:TPU:9, one launch (start us, length us, event | category | flops | bytes accessed | tf_op | source)
XLA Modules:
  0.0 37.3 jit_solution(663226312697181980)
XLA Ops:
  0.0 35.1 %shard_map.64 = f32[2,2,256,256]{3,2,1,0:T(8,128)} custom-call(s32[2,6]{1,0:T(2,128)} %bitcast.3, f32[2,2,128,128]{3,2,1,0:T(8,128)} %obj_hbm.1, f32[2,128,128]{2,1,0:T(8,128)} %probe_hbm.1, f32[128,128]{1,0:T(8,128)} %phase_hbm.1, f32[1,1,6,128,128]{4,3,2,1,0:T(8,128)} %meas_hbm.1, bf16[2,2,256,256]{3,2,1,0:T(8,128)(2,1)} %constant.2.clone.table_hbm), custom_call_target="tpu_custom_call" | custom-call | tf_op jit(solution)/shard_map/pallas_call | solution.py:416
  35.1 2.3 %copy.8 = f32[2,2,256,256]{3,2,1,0:T(8,128)} copy(f32[2,2,256,256]{3,2,1,0:T(8,128)} %shard_map.64) | data formatting | bytes 2097152
